TPU v7x, 32 devices: a whole 2x2x4 slice. The times are simulated.
32 devices in a mesh: groups: 2 (over x), expert: 8 (over z, y), dp: 2 (over core).
Axes of the slice: x: 2, y: 2, z: 4, core: 2. Of those that a mesh axis runs over, the one named last changes fastest.
Arguments:
- tokens: bfloat16 [4096, 2048], P(('groups', 'expert', 'dp')), parts along dimension 0, may hold values from -2 to 2
- grad_rows: bfloat16 [4096, 8, 1024], P(('groups', 'expert', 'dp')), parts along dimension 0, may hold values from -2 to 2
- routes: int32 [4096, 8], P(('groups', 'expert', 'dp')), parts along dimension 0, may hold values from 0 to 31, all different within a row; in each aligned block of 128 rows (0 to 127, 128 to 255, ...) at most 96 rows name the same one
- doc_ids: int32 [4096], P(('groups', 'expert', 'dp')), parts along dimension 0, may hold values from 0 to 127, as said below
- input_proj: bfloat16 [32, 64, 2048], P('expert'), may hold values from -0.125 to 0.125
- grad_proj: bfloat16 [32, 64, 1024], P('expert'), may hold values from -0.1875 to 0.1875
Outputs:
- doc_features: float32 [256, 4096], P(('groups', 'expert', 'dp')), parts along dimension 0
There are 2 independent parts, one for each index of `groups`. A program takes and returns all parts, laid end to end along the dimension named above; an argument that names none is the same for every part. Nothing has to cross between parts.
Inputs may be any that keep to these rules, and one draw needn't show every extreme that they name: `routes`: each row names 8 different experts. Within the rows of one device (aligned blocks of 128 tokens) no expert is named more than 96 times, and in every draw some expert is named exactly 96 times by one device. `doc_ids`: ids never fall along the tokens. The tokens of the device with index i along expert+dp (aligned blocks of 128 tokens) belong to documents i * 8 to (i + 1) * 8 - 1, each of which has at least one token.
All inputs are finite; a program needn't handle non-finite values.
Results may differ from a plain program's by a relative error of at most 0.0041.
Values may be sent and summed in bfloat16 or wider, within the bound.
A program may use at most 128 MiB of HBM per device.

v0:
```python
import jax
import jax.numpy as jnp
from jax import lax
from jax.sharding import PartitionSpec as P

DOC_DEV = 8


def slot_sources(routes, experts, capacity):
    pair_expert = routes.reshape(-1)
    pair_count = pair_expert.shape[0]
    onehot = (pair_expert[:, None] == jnp.arange(experts, dtype=jnp.int32)[None, :]).astype(
        jnp.int32
    )
    slot_rank = jnp.sum(jnp.cumsum(onehot, axis=0) * onehot, axis=1) - 1
    target = pair_expert * capacity + slot_rank
    empty_slots = jnp.full((experts * capacity,), -1, jnp.int32)
    return empty_slots.at[target].set(jnp.arange(pair_count, dtype=jnp.int32))


def shards(tokens, grad_rows, routes, doc_ids, input_proj, grad_proj):
    tok_count = tokens.shape[0]
    fanout = routes.shape[1]
    model_width = tokens.shape[1]
    hidden = grad_rows.shape[2]
    local_experts = input_proj.shape[0]
    proj_rank = input_proj.shape[1]
    experts = local_experts * lax.axis_size("expert")
    capacity = 3 * tok_count * fanout // experts
    source = slot_sources(routes, experts, capacity)
    filled = source >= 0
    safe_pair = jnp.maximum(source, 0)
    safe_token = safe_pair // fanout
    send_inputs = jnp.where(filled[:, None], tokens[safe_token], jnp.zeros((), jnp.bfloat16))
    send_inputs = send_inputs.reshape(experts, capacity, model_width)
    flat_grads = grad_rows.reshape(tok_count * fanout, hidden)
    send_grads = jnp.where(filled[:, None], flat_grads[safe_pair], jnp.zeros((), jnp.bfloat16))
    send_grads = send_grads.reshape(experts, capacity, hidden)
    slot_doc = jnp.where(filled, doc_ids[safe_token], -1).reshape(experts, capacity)
    inputs_part = lax.all_to_all(send_inputs, "expert", split_axis=0, concat_axis=0, tiled=True)
    grads_part = lax.all_to_all(send_grads, "expert", split_axis=0, concat_axis=0, tiled=True)
    docs_part = lax.all_to_all(slot_doc, "expert", split_axis=0, concat_axis=0, tiled=True)
    senders = inputs_part.shape[0] // local_experts
    slot_span = inputs_part.shape[1]
    shaped_in = inputs_part.reshape(senders, local_experts, slot_span, model_width)
    shaped_grad = grads_part.reshape(senders, local_experts, slot_span, hidden)
    proj_in = jnp.einsum(
        "oecd,erd->oecr", shaped_in, input_proj, preferred_element_type=jnp.float32
    )
    proj_grad = jnp.einsum(
        "oecf,erf->oecr", shaped_grad, grad_proj, preferred_element_type=jnp.float32
    )
    proj_in = proj_in.reshape(senders * local_experts, slot_span, proj_rank).astype(jnp.bfloat16)
    proj_grad = proj_grad.reshape(senders * local_experts, slot_span, proj_rank).astype(
        jnp.bfloat16
    )
    slot_total = proj_in.shape[0] * proj_in.shape[1]
    in_flat = proj_in.reshape(slot_total, proj_rank)
    grad_flat = proj_grad.reshape(slot_total, proj_rank)
    docs_flat = docs_part.reshape(slot_total)
    row_index = lax.axis_index("dp")
    row_count = lax.axis_size("dp")
    group = 2 * DOC_DEV
    turns = DOC_DEV * lax.axis_size("expert") // group

    def one_group(index):
        rows = index * group + jnp.arange(group, dtype=jnp.int32)
        wanted = (rows // DOC_DEV * row_count + row_index) * DOC_DEV + rows % DOC_DEV
        marks = (docs_flat[:, None] == wanted[None, :]).astype(jnp.bfloat16)
        left_side = (marks[:, :, None] * grad_flat[:, None, :]).reshape(
            slot_total, group * proj_rank
        )
        product = lax.dot_general(
            left_side, in_flat, (((0,), (0,)), ((), ())), preferred_element_type=jnp.float32
        )
        return product.reshape(group, proj_rank * proj_rank)

    return lax.psum_scatter(
        lax.map(one_group, jnp.arange(turns, dtype=jnp.int32)).reshape(
            DOC_DEV * lax.axis_size("expert"), proj_rank * proj_rank
        ),
        "expert",
        scatter_dimension=0,
        tiled=True,
    )


def solution(mesh):
    in_specs = (
        P(("groups", "expert", "dp"), None),
        P(("groups", "expert", "dp"), None, None),
        P(("groups", "expert", "dp"), None),
        P(("groups", "expert", "dp")),
        P("expert", None, None),
        P("expert", None, None),
    )
    out_specs = P(("groups", "expert", "dp"), None)
    return jax.shard_map(shards, mesh=mesh, in_specs=in_specs, out_specs=out_specs, check_vma=False)
```

profile of v0, /device:TPU:0, one launch (start us, length us, event | category | flops | bytes accessed | tf_op | source)
XLA Modules:
  0.0 589.5 jit_solution(3089020405185503890)
XLA Ops:
  6.5 0.9 copy.9
  7.7 0.7 broadcast_multiply_fusion.1
  8.4 9.0 %reduce-window.6 = s32[32,8,128]{2,1,0:T(8,128)S(1)} reduce-window(s32[32,8,128]{2,1,0:T(8,128)S(1)} %fusion.21, s32[]{:T(128)} %copy.46), window={size=1x1x128 pad=0_0x0_0x127_0}, to_apply=%region_0.0 | reduce-window | flops 4161536 | bytes 262148 | tf_op jit(solution)/shard_map/reduce-window
  18.1 4.3 scatter_custom_fusion
  22.5 18.7 %gather_fusion = s32[3072]{0:T(1024)S(1)} fusion(s32[128]{0:T(128)S(1)} %copy-done.2, s32[3072]{0:T(1024)S(1)} %get-tuple-element.122), kind=kCustom, calls=%fused_computation | custom fusion | bytes 36864 | tf_op jit(solution)/shard_map/gather | solution.py:39
  41.2 0.7 all_to_all.14
  41.9 7.3 %all-to-all-start = ((s32[8,4,96]{2,1,0:T(4,128)}), s32[8,4,96]{2,1,0:T(4,128)S(1)}, u32[]{:S(2)}, u32[]{:S(2)}) async-start(s32[8,4,96]{2,1,0:T(4,128)} %all_to_all.14), calls=%async_computation | async-start | bytes 32768 | tf_op jit(solution)/shard_map/all_to_all | solution.py:42
  49.2 13.9 %gather_fusion.1 = bf16[3072,1024]{1,0:T(8,128)(2,1)} fusion(bf16[1024,1024]{1,0:T(8,128)(2,1)S(1)} %bitcast.57, s32[3072]{0:T(1024)S(1)} %get-tuple-element.121), kind=kCustom, calls=%fused_computation.1 | custom fusion | bytes 12595200 | tf_op jit(solution)/shard_map/gather | solution.py:37
  63.1 6.6 %broadcast_select_fusion.1 = bf16[32,96,1024]{2,1,0:T(8,128)(2,1)} fusion(bf16[32,96,1024]{2,1,0:T(8,128)(2,1)} %bitcast.60, pred[32,96]{1,0:T(8,128)(4,1)S(1)} %broadcast_in_dim.57), kind=kLoop, calls=%fused_computation.18 | loop fusion | flops 3145728 | bytes 12585984 | tf_op jit(solution)/shard_map/jit(_where)/select_n | solution.py:37
  69.7 6.1 %all-to-all-start.1 = ((bf16[32,96,1024]{2,1,0:T(8,128)(2,1)}), bf16[32,96,1024]{2,1,0:T(8,128)(2,1)}, u32[]{:S(2)}, u32[]{:S(2)}) async-start(bf16[32,96,1024]{2,1,0:T(8,128)(2,1)} %broadcast_select_fusion.1), calls=%async_computation.1 | async-start | bytes 12582912 | tf_op jit(solution)/shard_map/all_to_all | solution.py:41
  75.9 15.9 %gather_fusion.2 = bf16[3072,2048]{1,0:T(8,128)(2,1)} fusion(bf16[128,2048]{1,0:T(8,128)(2,1)S(1)} %copy-done.3, s32[3072]{0:T(1024)S(1)} %get-tuple-element.122), kind=kCustom, calls=%fused_computation.2 | custom fusion | bytes 25178112 | tf_op jit(solution)/shard_map/gather | solution.py:34
  91.7 10.6 %broadcast_select_fusion = bf16[32,96,2048]{2,1,0:T(8,128)(2,1)} fusion(bf16[32,96,2048]{2,1,0:T(8,128)(2,1)} %bitcast.59, pred[32,96]{1,0:T(8,128)(4,1)S(1)} %broadcast_in_dim.57), kind=kLoop, calls=%fused_computation.15 | loop fusion | flops 6291456 | bytes 25168896 | tf_op jit(solution)/shard_map/jit(_where)/select_n | solution.py:34
  102.4 111.1 %all-to-all-done.1 = bf16[32,96,1024]{2,1,0:T(8,128)(2,1)} async-done(((bf16[32,96,1024]{2,1,0:T(8,128)(2,1)}), bf16[32,96,1024]{2,1,0:T(8,128)(2,1)}, u32[]{:S(2)}, u32[]{:S(2)}) %all-to-all-start.1) | async-done | bytes 6291488 | tf_op jit(solution)/shard_map/all_to_all | solution.py:41
  213.5 5.4 all-to-all-start.2
  219.2 5.2 fusion.14
  224.8 0.7 mul.88
  225.5 264.9 %all-to-all-done.2 = bf16[32,96,2048]{2,1,0:T(8,128)(2,1)} async-done(((bf16[32,96,2048]{2,1,0:T(8,128)(2,1)}), bf16[32,96,2048]{2,1,0:T(8,128)(2,1)}, u32[]{:S(2)}, u32[]{:S(2)}) %all-to-all-start.2) | async-done | bytes 12582944 | tf_op jit(solution)/shard_map/all_to_all | solution.py:40
  490.4 9.5 %fusion.11 = bf16[8,4,96,64]{2,3,0,1:T(8,128)(2,1)S(1)} fusion(bf16[8,4,96,2048]{3,2,1,0:T(8,128)(2,1)} %bitcast.15, bf16[4,64,2048]{2,1,0:T(8,128)(2,1)} %param.12), kind=kOutput, calls=%fused_computation.21 | convolution fusion | flops 805502976 | bytes 14024704 | tf_op jit(solution)/shard_map/oecd,erd->oecr/dot_general | solution.py:47
  500.2 18.5 %while.13 = (s32[]{:T(128)}, f32[4,16,4096]{2,1,0:T(8,128)}, s32[32,96]{1,0:T(8,128)}, s32[4]{0:T(128)S(1)}, s32[]{:T(128)}, /*index=5*/bf16[32,96,64]{1,0,2:T(8...) while((s32[]{:T(128)}, f32[4,16,4096]{2,1,0:T(8,128)}, ...), condition=%wide.wide.region_5.6_spmd, body=%wide.wide.region_4.5_spmd.sunk | while | flops 405897600 | bytes 14889741 | solution.py:79
  500.3 0.6 dynamic_slice.9
  502.2 1.8 fusion.40
  504.2 0.7 constant_dynamic-update-slice_fusion.3
  504.9 0.6 dynamic_slice.9
  506.8 1.8 fusion.40
  508.8 0.7 constant_dynamic-update-slice_fusion.3
  509.5 0.6 dynamic_slice.9
  511.4 1.8 fusion.40
  513.4 0.7 constant_dynamic-update-slice_fusion.3
  514.1 0.6 dynamic_slice.9
  516.1 1.8 fusion.40
  518.0 0.7 constant_dynamic-update-slice_fusion.3
  518.8 63.9 %reduce-scatter.2.cloned.1.call-done = f32[8,4096]{1,0:T(8,128)} async-done(((f32[64,4096]{1,0:T(8,128)}), f32[8,4096]{1,0:T(8,128)}) %reduce-scatter.2.cloned.1.call-update) | async-done | bytes 131088 | tf_op jit(solution)/shard_map/reduce_scatter | solution.py:78
  (57 shorter events, 5.4 us)
Async XLA Ops:
  6.5 42.7 %copy-start = (bf16[128,8,1024]{2,1,0:T(8,128)(2,1)S(1)}, bf16[128,8,1024]{2,1,0:T(8,128)(2,1)}, u32[]{:S(2)}) copy-start(bf16[128,8,1024]{2,1,0:T(8,128)(2,1)} %param.9) | copy-start | bytes 6291460
  6.5 16.0 %copy-start.2 = (s32[128]{0:T(128)S(1)}, s32[128]{0:T(128)}, u32[]{:S(2)}) copy-start(s32[128]{0:T(128)} %param.11) | copy-start | bytes 1540
  41.9 27.8 %all-to-all-start = ((s32[8,4,96]{2,1,0:T(4,128)}), s32[8,4,96]{2,1,0:T(4,128)S(1)}, u32[]{:S(2)}, u32[]{:S(2)}) async-start(s32[8,4,96]{2,1,0:T(4,128)} %all_to_all.14), calls=%async_computation | async-start | bytes 32768 | tf_op jit(solution)/shard_map/all_to_all | solution.py:42
  69.7 6.2 %copy-start.3 = (bf16[128,2048]{1,0:T(8,128)(2,1)S(1)}, bf16[128,2048]{1,0:T(8,128)(2,1)}, u32[]{:S(2)}) copy-start(bf16[128,2048]{1,0:T(8,128)(2,1)} %param.8) | copy-start | bytes 1572868
  69.7 149.4 %copy-start.5 = (s32[8,4,96]{2,1,0:T(4,128)}, s32[8,4,96]{2,1,0:T(4,128)S(1)}, u32[]{:S(2)}) copy-start(s32[8,4,96]{2,1,0:T(4,128)S(1)} %all-to-all-done) | copy-start | bytes 36868
  69.7 143.8 %all-to-all-start.1 = ((bf16[32,96,1024]{2,1,0:T(8,128)(2,1)}), bf16[32,96,1024]{2,1,0:T(8,128)(2,1)}, u32[]{:S(2)}, u32[]{:S(2)}) async-start(bf16[32,96,1024]{2,1,0:T(8,128)(2,1)} %broadcast_select_fusion.1), calls=%async_computation.1 | async-start | bytes 12582912 | tf_op jit(solution)/shard_map/all_to_all | solution.py:41
  102.4 116.9 %copy-start.6 = (bf16[4,64,1024]{2,1,0:T(8,128)(2,1)S(1)}, bf16[4,64,1024]{2,1,0:T(8,128)(2,1)}, u32[]{:S(2)}) copy-start(bf16[4,64,1024]{2,1,0:T(8,128)(2,1)} %param.13) | copy-start | bytes 1572868
  213.5 276.9 %all-to-all-start.2 = ((bf16[32,96,2048]{2,1,0:T(8,128)(2,1)}), bf16[32,96,2048]{2,1,0:T(8,128)(2,1)}, u32[]{:S(2)}, u32[]{:S(2)}) async-start(bf16[32,96,2048]{2,1,0:T(8,128)(2,1)} %broadcast_select_fusion), calls=%async_computation.2 | async-start | bytes 25165824 | tf_op jit(solution)/shard_map/all_to_all | solution.py:40
  218.9 363.8 %reduce-scatter.2.cloned.1.call-start = ((), (), s32[]{:S(2)}) async-start(), calls=%async_computation.4 | async-start | bytes 1179648 | tf_op jit(solution)/shard_map/reduce_scatter | solution.py:78
  224.8 275.1 %copy-start.4 = (bf16[32,96,64]{1,0,2:T(8,128)(2,1)}, bf16[32,96,64]{1,0,2:T(8,128)(2,1)S(1)}, u32[]{:S(2)}) copy-start(bf16[32,96,64]{1,0,2:T(8,128)(2,1)S(1)} %copy.17) | copy-start | bytes 1179652
  518.8 63.9 %copy-start.1 = (bf16[128,8,1024]{2,1,0:T(8,128)(2,1)S(1)}, bf16[128,8,1024]{2,1,0:T(8,128)(2,1)}, u32[]{:S(2)}) copy-start(bf16[128,8,1024]{2,1,0:T(8,128)(2,1)} %param.9) | copy-start | bytes 6291460
Sparse Core Ops, SparseCore 0:
  518.9 63.6 reduce-scatter.1
where the time goes:
time: 590 us
  waiting for transfers between devices  440 us (75%)
  local copies, waits for them, and re-layouts  62.9 us (11%)
  other arithmetic  29.7 us (5%)
  matrix products  21.8 us (4%)
  starting transfers between devices  19 us (3%)
  between operations  13.6 us (2%)
    all_to_all x1, waiting for transfers between devices, shards(): lax.all_to_all(send_inputs, 'expert', split_axis=0, concat_axis=0, tiled=...  265 us
    all_to_all x1, waiting for transfers between devices, shards(): lax.all_to_all(send_grads, 'expert', split_axis=0, concat_axis=0, tiled=T...  111 us
    reduce_scatter x1, waiting for transfers between devices, shards(): lax.psum_scatter(lax.map(one_group, jnp.arange(turns, dtype=jnp.int32)).r...  63.9 us
    gather x1, local copies, waits for them, and re-layouts, shards(): doc_ids[safe_token]  18.7 us
    gather x1, local copies, waits for them, and re-layouts, shards(): tokens[safe_token]  15.9 us
    gather x1, local copies, waits for them, and re-layouts, shards(): flat_grads[safe_pair]  13.9 us
  transfers between devices with their start and end apart: 4, of which 3 were waited for; matrix products, arithmetic and copies ran while one was open for 9% of the time, Pallas kernels for 0%

commit v1 on v0

v1 whole, which is shorter than its diff:
```python
import jax
import jax.numpy as jnp
from jax import lax
from jax.sharding import PartitionSpec as P

DOC_DEV = 8


def shards(tokens, grad_rows, routes, doc_ids, input_proj, grad_proj):
    tok, fan = routes.shape
    rank = input_proj.shape[1]
    local = input_proj.shape[0]
    experts = local * lax.axis_size("expert")
    core = lax.axis_index("dp")
    half = local // lax.axis_size("dp")

    def gather(w):
        mine = lax.dynamic_slice_in_dim(w, core * half, half, 0)
        part = lax.all_gather(mine, "expert", axis=0)
        both = lax.all_gather(part, "dp", axis=1)
        return both.reshape((experts * rank, w.shape[2]))

    w_in = gather(input_proj)
    w_gr = gather(grad_proj)
    dense_in = jnp.einsum("td,nd->tn", tokens, w_in, preferred_element_type=jnp.float32)
    dense_in = dense_in.astype(jnp.bfloat16).reshape(tok, experts, rank)
    flat = grad_rows.reshape(tok * fan, grad_rows.shape[2])
    dense_gr = jnp.einsum("pf,nf->pn", flat, w_gr, preferred_element_type=jnp.float32)
    dense_gr = dense_gr.reshape(tok, fan, experts, rank)
    pick = routes[:, :, None] == jnp.arange(experts, dtype=jnp.int32)
    feat_gr = jnp.sum(jnp.where(pick[..., None], dense_gr, 0.0), axis=2).astype(jnp.bfloat16)
    feat_in = jnp.einsum("tke,ter->tkr", pick.astype(jnp.bfloat16), dense_in,
                         preferred_element_type=jnp.float32).astype(jnp.bfloat16)
    first = (lax.axis_index("expert") * lax.axis_size("dp") + core) * DOC_DEV
    marks = ((doc_ids - first)[:, None] == jnp.arange(DOC_DEV, dtype=jnp.int32)).astype(jnp.bfloat16)
    left = marks[:, None, :, None] * feat_gr[:, :, None, :]
    out = lax.dot_general(left.reshape(tok * fan, DOC_DEV * rank), feat_in.reshape(tok * fan, rank),
                          (((0,), (0,)), ((), ())), preferred_element_type=jnp.float32)
    return out.reshape(DOC_DEV, rank * rank)


def solution(mesh):
    in_specs = (
        P(("groups", "expert", "dp"), None),
        P(("groups", "expert", "dp"), None, None),
        P(("groups", "expert", "dp"), None),
        P(("groups", "expert", "dp")),
        P("expert", None, None),
        P("expert", None, None),
    )
    out_specs = P(("groups", "expert", "dp"), None)
    return jax.shard_map(shards, mesh=mesh, in_specs=in_specs, out_specs=out_specs, check_vma=False)
```

time: 590 us -> 215 us (0.36)
  waiting for transfers between devices: 440 us -> 138 us
  local copies, waits for them, and re-layouts: 62.9 us -> 35.5 us
  other arithmetic: 29.7 us -> 9.61 us
  starting transfers between devices: 19 us -> 0.12 us
    all_to_all x3 -> x0, waiting for transfers between devices: 376 us -> none  [the longest x1 265 us: shards(): lax.all_to_all(send_inputs, 'expert', split_axis=0, concat_axis=0, tiled=...]
    all_gather x0 -> x4, waiting for transfers between devices: none -> 138 us  [the longest x2 125 us: gather(): part = lax.all_gather(mine, 'expert', axis=0)]
    reduce_scatter x1 -> x0, waiting for transfers between devices: 63.9 us -> none  [shards(): lax.psum_scatter(lax.map(one_group, jnp.arange(turns, dtype=jnp.int32)).r...]
    gather x3 -> x0, local copies, waits for them, and re-layouts: 48.4 us -> none  [the longest x1 18.7 us: shards(): doc_ids[safe_token]]
    all_to_all x3 -> x0, starting transfers between devices: 18.8 us -> none  [the longest x1 7.28 us: shards(): lax.all_to_all(slot_doc, 'expert', split_axis=0, concat_axis=0, tiled=True)]
    reshape x0 -> x3, local copies, waits for them, and re-layouts: none -> 18.5 us  [the longest x1 14.4 us: shards(): dense_gr = dense_gr.reshape(tok, fan, experts, rank)]
    select_n x4 -> x0, other arithmetic: 17.2 us -> none  [the longest x1 10.6 us: shards(): jnp.where(filled[:, None], tokens[safe_token], jnp.zeros((), jnp.bfloat16))]
    dot_general x0 -> x1, local copies, waits for them, and re-layouts: none -> 9.97 us  [shards(): jnp.einsum('pf,nf->pn', flat, w_gr, preferred_element_type=jnp.float32)]
  transfers between devices with their start and end apart: 4 -> 4, of which waited for: 3 -> 3; matrix products, arithmetic and copies ran while one was open for 9% -> 22% of each run, Pallas kernels for 0% -> 0%
where the time goes in v1:
time: 215 us; the launch traced here: 214 us
  waiting for transfers between devices  138 us (64%)
  local copies, waits for them, and re-layouts  35.5 us (17%)
  matrix products  17.6 us (8%)
  between operations  13.2 us (6%)
  other arithmetic  9.61 us (4%)
    all_gather x2, waiting for transfers between devices, gather(): part = lax.all_gather(mine, 'expert', axis=0)  125 us
    reshape x1, local copies, waits for them, and re-layouts, shards(): dense_gr = dense_gr.reshape(tok, fan, experts, rank)  14.4 us
    all_gather x2, waiting for transfers between devices, gather(): both = lax.all_gather(part, 'dp', axis=1)  13.1 us
    dot_general x1, local copies, waits for them, and re-layouts, shards(): jnp.einsum('pf,nf->pn', flat, w_gr, preferred_element_type=jnp.float32)  9.97 us
    dot_general x1, matrix products, shards(): jnp.einsum('pf,nf->pn', flat, w_gr, preferred_element_type=jnp.float32)  8.98 us
    reduce_sum x1, other arithmetic, shards(): jnp.sum(jnp.where(pick[..., None], dense_gr, 0.0), axis=2)  7.63 us
    dot_general x1, matrix products, shards(): jnp.einsum('td,nd->tn', tokens, w_in, preferred_element_type=jnp.float32)  6.6 us
  transfers between devices with their start and end apart: 4, of which 3 were waited for; matrix products, arithmetic and copies ran while one was open for 22% of the time, Pallas kernels for 0%

profile of v1, /device:TPU:0, one launch (start us, length us, event | category | flops | bytes accessed | tf_op | source)
XLA Modules:
  0.0 214.2 jit_solution(268778559178705322)
XLA Ops:
  6.5 0.0 copy-start
  6.5 0.0 all-gather.9.cloned.1.call-start
  6.5 1.8 constant_dynamic-slice_fusion.1
  8.3 0.0 copy-start.1
  8.4 0.0 all-gather.9.cloned.1.call-update
  8.4 0.0 all-gather.13.cloned.1.call-start
  8.4 1.9 constant_dynamic-slice_fusion
  10.3 0.0 all-gather.13.cloned.1.call-update
  10.3 0.0 all-gather.11.cloned.1.call-start
  10.4 51.1 %all-gather.9.cloned.1.call-done = bf16[16,64,1024]{2,1,0:T(8,128)(2,1)} async-done(((bf16[2,64,1024]{2,1,0:T(8,128)(2,1)}), bf16[16,64,1024]{2,1,0:T(8,128)(2,1)}) %all-gather.9.cloned.1.call-update) | async-done | bytes 2097168 | tf_op jit(solution)/shard_map/all_gather | solution.py:19
  61.5 0.0 all-gather.11.cloned.1.call-update
  61.5 0.0 all-gather.15.cloned.1.call-start
  61.6 74.0 %all-gather.13.cloned.1.call-done = bf16[16,64,2048]{2,1,0:T(8,128)(2,1)} async-done(((bf16[2,64,2048]{2,1,0:T(8,128)(2,1)}), bf16[16,64,2048]{2,1,0:T(8,128)(2,1)}) %all-gather.13.cloned.1.call-update) | async-done | bytes 4194320 | tf_op jit(solution)/shard_map/all_gather | solution.py:19
  135.6 0.0 all-gather.15.cloned.1.call-update
  135.6 0.0 copy-done.1
  135.6 0.1 copy.14
  135.7 0.0 copy-done.2
  135.7 0.1 fusion.3
  135.8 0.2 iota_compare_fusion
  136.0 13.1 %all-gather.11.cloned.1.call-done = bf16[8,4,64,1024]{3,2,1,0:T(8,128)(2,1)} async-done(((bf16[8,2,64,1024]{3,2,1,0:T(8,128)(2,1)}), bf16[8,4,64,1024]{3,2,1,0:T(8,128)(2,1)}) %all-gather.11.cloned.1.call-update) | async-done | bytes 4194320 | tf_op jit(solution)/shard_map/all_gather | solution.py:20
  149.1 0.0 copy-done
  149.1 9.0 %convolution_bitcast_fusion = f32[1024,2048]{0,1:T(8,128)} fusion(bf16[2048,1024]{1,0:T(8,128)(2,1)} %bitcast.27, bf16[128,8,1024]{2,1,0:T(8,128)(2,1)S(1)} %copy-done), kind=kOutput, calls=%fused_computation.1 | convolution fusion | flops 4294967296 | bytes 14680064 | tf_op jit(solution)/shard_map/pf,nf->pn/dot_general | solution.py:28
  158.1 10.0 %copy.15 = f32[1024,2048]{1,0:T(8,128)} copy(f32[1024,2048]{0,1:T(8,128)} %convolution_bitcast_fusion) | data formatting | bytes 16777216 | tf_op jit(solution)/shard_map/pf,nf->pn/dot_general | solution.py:28
  168.0 14.4 %reshape.64 = f32[128,8,32,64]{3,2,1,0:T(8,128)} reshape(f32[1024,2048]{1,0:T(8,128)} %copy.15) | data formatting | bytes 16777216 | tf_op jit(solution)/shard_map/reshape | solution.py:29
  182.4 7.6 %select_reduce_fusion = bf16[128,8,64]{2,1,0:T(8,128)(2,1)S(1)} fusion(f32[128,8,32,64]{3,2,1,0:T(8,128)} %reshape.64, pred[128,8,32]{2,1,0:T(8,128)(4,1)S(1)} %iota_compare_fusion), kind=kLoop, calls=%fused_computation | loop fusion | flops 4128768 | bytes 8552448 | tf_op jit(solution)/shard_map/reduce_sum | solution.py:31
  190.1 1.7 broadcast_multiply_fusion
  191.8 3.2 %mul.39 = bf16[1024,512]{1,0:T(8,128)(2,1)S(1)} reshape(bf16[128,8,8,64]{3,2,1,0:T(8,128)(2,1)} %broadcast_multiply_fusion) | data formatting | bytes 2097152 | tf_op jit(solution)/shard_map/mul | solution.py:36
  195.0 0.0 all-gather.15.cloned.1.call-done
  195.0 6.6 %convolution_convert_fusion = bf16[2048,128]{1,0:T(8,128)(2,1)} fusion(bf16[2048,2048]{1,0:T(8,128)(2,1)} %bitcast.26, bf16[128,2048]{1,0:T(8,128)(2,1)} %param.6), kind=kOutput, calls=%fused_computation.2 | convolution fusion | flops 1074003968 | bytes 9437184 | tf_op jit(solution)/shard_map/td,nd->tn/dot_general | solution.py:25
  201.6 3.3 %copy.16 = bf16[128,32,64]{2,1,0:T(8,128)(2,1)} copy(bf16[128,32,64]{0,2,1:T(8,128)(2,1)} %bitcast.25) | data formatting | bytes 1048576 | tf_op jit(solution)/shard_map/reshape | solution.py:26
  204.9 2.0 fusion.2
  206.9 0.8 reshape.68
  (2 shorter events, 0.0 us)
Async XLA Ops:
  6.5 142.5 %copy-start = (bf16[128,8,1024]{2,1,0:T(8,128)(2,1)S(1)}, bf16[128,8,1024]{2,1,0:T(8,128)(2,1)}, u32[]{:S(2)}) copy-start(bf16[128,8,1024]{2,1,0:T(8,128)(2,1)} %param.7) | copy-start | bytes 6291460
  6.5 55.0 %all-gather.9.cloned.1.call-start = ((), (), s32[]{:S(2)}) async-start(), calls=%async_computation | async-start | bytes 2359296 | tf_op jit(solution)/shard_map/all_gather | solution.py:19
  8.3 127.2 %copy-start.1 = (s32[128,8]{0,1:T(8,128)S(1)}, s32[128,8]{0,1:T(8,128)}, u32[]{:S(2)}) copy-start(s32[128,8]{0,1:T(8,128)} %param.8) | copy-start | bytes 12292
  8.3 127.3 %copy-start.2 = (s32[128]{0:T(128)S(1)}, s32[128]{0:T(128)}, u32[]{:S(2)}) copy-start(s32[128]{0:T(128)} %param.9) | copy-start | bytes 1540
  8.4 127.2 %all-gather.13.cloned.1.call-start = ((), (), s32[]{:S(2)}) async-start(), calls=%async_computation.2 | async-start | bytes 4718592 | tf_op jit(solution)/shard_map/all_gather | solution.py:19
  10.3 138.7 %all-gather.11.cloned.1.call-start = ((), (), s32[]{:S(2)}) async-start(), calls=%async_computation.1 | async-start | bytes 6291456 | tf_op jit(solution)/shard_map/all_gather | solution.py:20
  61.5 133.4 %all-gather.15.cloned.1.call-start = ((), (), s32[]{:S(2)}) async-start(), calls=%async_computation.3 | async-start | bytes 12582912 | tf_op jit(solution)/shard_map/all_gather | solution.py:20
Sparse Core Ops, SparseCore 0:
  9.5 51.9 all-gather.8
  63.6 71.8 all-gather.12
  137.1 11.9 all-gather.10
  150.5 21.0 all-gather.14

commit v2 on v1

v2 whole, which is shorter than its diff:
```python
import functools

import jax
import jax.numpy as jnp
from jax import lax
from jax.experimental import pallas as pl
from jax.experimental.pallas import tpu as pltpu
from jax.sharding import PartitionSpec as P

DOC_DEV = 8
MESH = pl.DeviceIdType.MESH
LO, HI, XP, CORE, YP = range(5)
NT = (((1,), (1,)), ((), ()))
FULL_IN = (1,)


def kernel(zn, yn, tok_hbm, grad_hbm, routes_ref, doc_ref, win_hbm, wgr_hbm, out_ref,
           tok, grads, win, wgr, feat_send, feat_recv, acc_in, acc_gr, route_at,
           local_sem, in_recv, gr_recv, in_send, gr_send,
           tok_send_sem, tok_recv_sem, feat_send_sem, feat_recv_sem):
    group = lax.axis_index("groups")
    place = lax.axis_index("expert")
    core = lax.axis_index("dp")
    z, y = place // yn, place % yn
    hx = group % 2
    tokens = tok_hbm.shape[0]
    pairs = grad_hbm.shape[0]
    cols = win.shape[1]
    part = cols // 4
    last = zn - 1
    to = {
        LO: {"expert": place - yn},
        HI: {"expert": place + yn},
        XP: {"groups": group + 1 - 2 * hx},
        CORE: {"dp": 1 - core},
    }
    if yn == 2:
        to[YP] = {"expert": place + 1 - 2 * y}

    def have(link):
        if link == LO:
            return z > 0
        if link == HI:
            return z < last
        return None

    def when(conds, fn):
        conds = [c for c in conds if c is not None]
        if not conds:
            fn()
            return
        both = conds[0]
        for c in conds[1:]:
            both = jnp.logical_and(both, c)
        pl.when(both)(fn)

    def valid(d, sign):
        if d == 0:
            return None
        return z + d <= last if sign > 0 else z - d >= 0

    slot_own = z * yn + y
    local = [
        pltpu.make_async_copy(tok_hbm, tok.at[pl.ds(0, tokens)], local_sem.at[0]),
        pltpu.make_async_copy(wgr_hbm, wgr.at[slot_own], local_sem.at[1]),
        pltpu.make_async_copy(grad_hbm, grads, local_sem.at[2]),
        pltpu.make_async_copy(win_hbm, win.at[z], local_sem.at[3]),
    ]
    for c in local:
        c.start()

    barrier = pltpu.get_barrier_semaphore()
    for link in to:
        def greet(link=link):
            pl.semaphore_signal(barrier, inc=1, device_id=to[link], device_id_type=MESH)
        when([have(link)], greet)
    inner = (z > 0).astype(jnp.int32) + (z < last).astype(jnp.int32)
    pl.semaphore_wait(barrier, len(to) - 2 + inner)

    sent = []

    def send(make, conds):
        when(conds, lambda: make().start())
        sent.append((make, conds))

    def rows_of(dh, dc=0):
        half = hx if dh == 0 else 1 - hx
        which = core if dc == 0 else 1 - core
        return pl.ds(pl.multiple_of((half * 2 + which) * part, part), part), half * 2 + which

    def pack(kind, d, sign, yr):
        zz = z + sign * d
        if kind == "in":
            return win, zz, in_send, in_recv
        yy = y if yr == 0 else 1 - y
        return wgr, zz * yn + yy, gr_send, gr_recv

    def send_piece(kind, d, sign, yr, dh, link):
        buf, slot, ssem, rsem = pack(kind, d, sign, yr)
        rows, number = rows_of(dh)
        if d == 0 and yr == 0:
            src = (win_hbm if kind == "in" else wgr_hbm).at[rows]
        else:
            src = buf.at[slot, rows]

        def make():
            return pltpu.make_async_remote_copy(
                src_ref=src, dst_ref=buf.at[slot, rows],
                send_sem=ssem.at[link, slot, dh], recv_sem=rsem.at[slot, number],
                device_id=to[link], device_id_type=MESH)
        send(make, [valid(d, sign), have(link)])

    def arrive(kind, d, sign, yr, dh, dc=0):
        buf, slot, ssem, rsem = pack(kind, d, sign, yr)
        rows, number = rows_of(dh, dc)

        def wait():
            pltpu.make_async_remote_copy(
                src_ref=buf.at[slot, rows], dst_ref=buf.at[slot, rows],
                send_sem=ssem.at[CORE, slot, dh], recv_sem=rsem.at[slot, number],
                device_id=to[CORE], device_id_type=MESH).wait_recv()
        when([valid(d, sign)], wait)

    def z_event(kind, d, sign):
        link = LO if sign > 0 else HI
        arrive(kind, d, sign, 0, 0)
        if d < last:
            send_piece(kind, d, sign, 0, 0, link)
        full = kind == "in" and d in FULL_IN
        if kind == "gr" and yn == 2:
            send_piece(kind, d, sign, 0, 0, YP)
        if not full:
            send_piece(kind, d, sign, 0, 0, XP)
        send_piece(kind, d, sign, 0, 0, CORE)
        if full:
            arrive(kind, d, sign, 0, 1)
            if d < last and d + 1 in FULL_IN:
                send_piece(kind, d, sign, 0, 1, link)
            send_piece(kind, d, sign, 0, 1, CORE)

    def y_event(d, sign):
        arrive("gr", d, sign, 1, 0)
        if d > 0:
            send_piece("gr", d, sign, 1, 0, XP)
        send_piece("gr", d, sign, 1, 0, CORE)
        if d == 0:
            arrive("gr", d, sign, 1, 1)
            send_piece("gr", d, sign, 1, 1, CORE)

    def x_event(kind, d, sign, yr):
        if kind == "in" and d in FULL_IN:
            return
        arrive(kind, d, sign, yr, 1)
        if kind == "in" and d < last and d + 1 in FULL_IN:
            send_piece(kind, d, sign, yr, 1, LO if sign > 0 else HI)
        send_piece(kind, d, sign, yr, 1, CORE)

    def core_event(kind, d, sign, yr):
        arrive(kind, d, sign, yr, 0, 1)
        arrive(kind, d, sign, yr, 1, 1)

    tile = 256

    def select(acc, at, slot, value):
        hit = route_at[pl.ds(at, tile), :]
        acc[pl.ds(at, tile), :] = jnp.where(
            hit == 4 * slot, value[:, :128],
            jnp.where(hit == 4 * slot + 2, value[:, 128:], acc[pl.ds(at, tile), :]))

    def project_grads(d, sign, yr):
        _, slot, _, _ = pack("gr", d, sign, yr)

        def run():
            @pl.loop(0, pairs // tile)
            def _(i):
                at = pl.multiple_of(i * tile, tile)
                value = lax.dot_general(grads[pl.ds(at, tile), :], wgr[slot], NT,
                                        preferred_element_type=jnp.float32)
                select(acc_gr, at, slot, value)
        when([valid(d, sign)], run)

    fan = pairs // tokens

    def select_inputs(slot, block):
        @pl.loop(0, pairs // tile)
        def _(i):
            at = pl.multiple_of(i * tile, tile)
            few = tile // fan
            value = block[pl.ds(pl.multiple_of(i * few, few), few), :].astype(jnp.float32)
            value = jnp.broadcast_to(value[:, None, :], (few, fan, cols)).reshape(tile, cols)
            select(acc_in, at, slot, value)

    def project_inputs(d, sign):
        _, slot, _, _ = pack("in", d, sign, 0)

        def run():
            value = lax.dot_general(tok[...], win[slot], NT, preferred_element_type=jnp.float32)
            feat_send[slot] = value.astype(jnp.bfloat16)
        when([valid(d, sign)], run)
        if yn == 2:
            def make():
                return pltpu.make_async_remote_copy(
                    src_ref=feat_send.at[slot, pl.ds(tokens, tokens)], dst_ref=feat_recv.at[slot],
                    send_sem=feat_send_sem.at[slot], recv_sem=feat_recv_sem.at[slot],
                    device_id=to[YP], device_id_type=MESH)
            send(make, [valid(d, sign)])
        when([valid(d, sign)], lambda: select_inputs(slot * yn + y, feat_send.at[slot]))

    def features_back(d, sign):
        if yn == 1:
            return
        _, slot, _, _ = pack("in", d, sign, 0)

        def run():
            pltpu.make_async_remote_copy(
                src_ref=feat_recv.at[slot], dst_ref=feat_recv.at[slot],
                send_sem=feat_send_sem.at[slot], recv_sem=feat_recv_sem.at[slot],
                device_id=to[YP], device_id_type=MESH).wait_recv()
            select_inputs(slot * yn + 1 - y, feat_recv.at[slot])
        when([valid(d, sign)], run)

    for link in (LO, HI):
        send_piece("gr", 0, 1, 0, 0, link)
        send_piece("in", 0, 1, 0, 0, link)
        if 1 in FULL_IN:
            send_piece("in", 0, 1, 0, 1, link)
    if yn == 2:
        def make_tok():
            return pltpu.make_async_remote_copy(
                src_ref=tok_hbm, dst_ref=tok.at[pl.ds(tokens, tokens)],
                send_sem=tok_send_sem, recv_sem=tok_recv_sem,
                device_id=to[YP], device_id_type=MESH)
        send(make_tok, [])
        send_piece("gr", 0, 1, 0, 0, YP)
        send_piece("gr", 0, 1, 0, 1, YP)

    pair = lax.broadcasted_iota(jnp.int32, (pairs, tokens), 0) // fan
    spread = (pair == lax.broadcasted_iota(jnp.int32, (pairs, tokens), 1)).astype(jnp.bfloat16)
    named = jnp.dot(spread, routes_ref[...].astype(jnp.bfloat16), preferred_element_type=jnp.float32)
    choice = lax.broadcasted_iota(jnp.int32, (pairs, fan), 0) % fan
    mine = choice == lax.broadcasted_iota(jnp.int32, (pairs, fan), 1)
    named = jnp.sum(jnp.where(mine, named, 0.0), axis=1, keepdims=True).astype(jnp.int32)
    half_of = lax.broadcasted_iota(jnp.int32, (pairs, 128), 1) // 64
    route_at[...] = named - half_of
    acc_in[...] = jnp.zeros_like(acc_in)
    acc_gr[...] = jnp.zeros_like(acc_gr)
    for c in local:
        c.wait()

    signs = (1, -1)
    other = tuple(range(1, yn))
    project_grads(0, 1, 0)
    for d in range(1, zn):
        for s in signs:
            z_event("gr", d, s)
        if d > 1:
            for s in signs:
                x_event("in", d - 1, s, 0)
        for s in signs:
            z_event("in", d, s)
        if d == 1:
            if yn == 2:
                make_tok().wait_recv()
            project_inputs(0, 1)
            if yn == 2:
                y_event(0, 1)
                core_event("gr", 0, 1, 1)
                project_grads(0, 1, 1)
            features_back(0, 1)
        for s in signs:
            x_event("gr", d, s, 0)
        for e in other:
            for s in signs:
                y_event(d, s)
        if d > 1:
            for s in signs:
                core_event("in", d - 1, s, 0)
                project_inputs(d - 1, s)
            for s in signs:
                core_event("gr", d - 1, s, 0)
                project_grads(d - 1, s, 0)
            for e in other:
                for s in signs:
                    x_event("gr", d - 1, s, e)
            for e in other:
                for s in signs:
                    core_event("gr", d - 1, s, e)
                    project_grads(d - 1, s, e)
            for s in signs:
                features_back(d - 1, s)
    for s in signs:
        x_event("in", last, s, 0)
    for e in other:
        for s in signs:
            x_event("gr", last, s, e)
    for s in signs:
        core_event("gr", last, s, 0)
        project_grads(last, s, 0)
    for s in signs:
        core_event("in", last, s, 0)
        project_inputs(last, s)
    for e in other:
        for s in signs:
            core_event("gr", last, s, e)
            project_grads(last, s, e)
    for s in signs:
        features_back(last, s)

    right = acc_in[...]
    right = (right + pltpu.roll(right, 64, 1)).astype(jnp.bfloat16)
    left = acc_gr[...]
    left = (left + pltpu.roll(left, 64, 1)).astype(jnp.bfloat16).astype(jnp.float32)
    left = left.T
    docs = out_ref.shape[0]
    first = (place * lax.axis_size("dp") + core) * docs
    own_doc = jnp.broadcast_to(doc_ref[...] - first, (docs, tokens)).astype(jnp.bfloat16)
    pair = lax.broadcasted_iota(jnp.int32, (tokens, pairs), 1) // fan
    spread = (pair == lax.broadcasted_iota(jnp.int32, (tokens, pairs), 0)).astype(jnp.bfloat16)
    pair_doc = jnp.dot(own_doc, spread, preferred_element_type=jnp.float32).astype(jnp.int32)
    marks = pair_doc == lax.broadcasted_iota(jnp.int32, (docs, pairs), 0)
    low = lax.broadcasted_iota(jnp.int32, (docs, 128), 1) < 64
    step = 16
    for a in range(0, 64, step):
        block = jnp.broadcast_to(left[a:a + step][:, None, :], (step, docs, pairs))
        block = jnp.where(marks[None], block, 0.0).reshape(step * docs, pairs)
        got = jnp.dot(block.astype(jnp.bfloat16), right, preferred_element_type=jnp.float32)
        for j in range(0, step, 2):
            at = (a + j) * 64
            out_ref[:, at:at + 128] = jnp.where(
                low, got[j * docs:(j + 1) * docs], got[(j + 1) * docs:(j + 2) * docs])

    for make, conds in sent:
        when(conds, lambda: make().wait_send())


def shards(yn, tokens, grad_rows, routes, doc_ids, input_proj, grad_proj):
    tok, fan = routes.shape
    local, rank, width = input_proj.shape
    hidden = grad_proj.shape[2]
    zn = lax.axis_size("expert") // yn
    cols = local * rank
    pairs = tok * fan
    vmem = pl.BlockSpec(memory_space=pltpu.VMEM)
    hbm = pl.BlockSpec(memory_space=pl.ANY)
    dma = pltpu.SemaphoreType.DMA
    return pl.pallas_call(
        functools.partial(kernel, zn, yn),
        out_shape=jax.ShapeDtypeStruct((DOC_DEV, rank * rank), jnp.float32),
        in_specs=[hbm, hbm, vmem, vmem, hbm, hbm],
        out_specs=vmem,
        scratch_shapes=[
            pltpu.VMEM((yn * tok, width), jnp.bfloat16),
            pltpu.VMEM((pairs, hidden), jnp.bfloat16),
            pltpu.VMEM((zn, cols, width), jnp.bfloat16),
            pltpu.VMEM((zn * yn, cols, hidden), jnp.bfloat16),
            pltpu.VMEM((zn, yn * tok, cols), jnp.bfloat16),
            pltpu.VMEM((zn, tok, cols), jnp.bfloat16),
            pltpu.VMEM((pairs, 128), jnp.float32),
            pltpu.VMEM((pairs, 128), jnp.float32),
            pltpu.VMEM((pairs, 128), jnp.int32),
            dma((4,)),
            dma((zn, 4)),
            dma((zn * yn, 4)),
            dma((4, zn, 2)),
            dma((5, zn * yn, 2)),
            dma,
            dma,
            dma((zn,)),
            dma((zn,)),
        ],
        compiler_params=pltpu.CompilerParams(
            collective_id=0, has_side_effects=True, vmem_limit_bytes=56 * 2**20),
        cost_estimate=pl.CostEstimate(
            flops=2 * pairs * hidden * cols * zn * yn + 2 * tok * yn * width * cols * zn,
            bytes_accessed=16 * 2**20, transcendentals=0),
        name="project_and_sum",
    )(tokens, grad_rows.reshape(pairs, hidden), routes, doc_ids.reshape(1, tok),
      input_proj.reshape(cols, width), grad_proj.reshape(cols, hidden))


def solution(mesh):
    in_specs = (
        P(("groups", "expert", "dp"), None),
        P(("groups", "expert", "dp"), None, None),
        P(("groups", "expert", "dp"), None),
        P(("groups", "expert", "dp")),
        P("expert", None, None),
        P("expert", None, None),
    )
    out_specs = P(("groups", "expert", "dp"), None)
    yn = 2 if mesh.shape["expert"] == 8 else 1
    return jax.shard_map(functools.partial(shards, yn), mesh=mesh, in_specs=in_specs,
                         out_specs=out_specs, check_vma=False)
```

time: 215 us -> 65.6 us (0.31)
  waiting for transfers between devices: 138 us -> 0 us
  Pallas kernels: 0 us -> 62.4 us
  local copies, waits for them, and re-layouts: 35.5 us -> 2.98 us
  matrix products: 17.6 us -> 0 us
  between operations: 13.2 us -> 0.01 us
  other arithmetic: 9.61 us -> 0 us
    all_gather x4 -> x0, waiting for transfers between devices: 138 us -> none  [the longest x2 125 us: gather(): part = lax.all_gather(mine, 'expert', axis=0)]
    pallas_call x0 -> x1, Pallas kernels: none -> 62.4 us  [shards(): pl.pallas_call(functools.partial(kernel, zn, yn), out_shape=jax.ShapeDtyp...]
    reshape x3 -> x0, local copies, waits for them, and re-layouts: 18.5 us -> none  [the longest x1 14.4 us: shards(): dense_gr = dense_gr.reshape(tok, fan, experts, rank)]
    dot_general x3 -> x0, matrix products: 17.6 us -> none  [the longest x1 8.98 us: shards(): jnp.einsum('pf,nf->pn', flat, w_gr, preferred_element_type=jnp.float32)]
    dot_general x1 -> x0, local copies, waits for them, and re-layouts: 9.97 us -> none  [shards(): jnp.einsum('pf,nf->pn', flat, w_gr, preferred_element_type=jnp.float32)]
    reduce_sum x1 -> x0, other arithmetic: 7.63 us -> none  [shards(): jnp.sum(jnp.where(pick[..., None], dense_gr, 0.0), axis=2)]
    dynamic_slice x2 -> x0, local copies, waits for them, and re-layouts: 3.7 us -> none  [gather(): mine = lax.dynamic_slice_in_dim(w, core * half, half, 0)]
    mul x1 -> x0, local copies, waits for them, and re-layouts: 3.19 us -> none  [shards(): left = marks[:, None, :, None] * feat_gr[:, :, None, :]]
  transfers between devices with their start and end apart: 4 -> 0, of which waited for: 3 -> 0; matrix products, arithmetic and copies ran while one was open for 22% -> 0% of each run, Pallas kernels for 0% -> 0%
where the time goes in v2:
time: 65.6 us; the launch traced here: 65.4 us
  Pallas kernels  62.4 us (95%)
  local copies, waits for them, and re-layouts  2.98 us (5%)
    pallas_call x1, Pallas kernels, shards(): pl.pallas_call(functools.partial(kernel, zn, yn), out_shape=jax.ShapeDtyp...  62.4 us
    unnamed x2, local copies, waits for them, and re-layouts  2.98 us

profile of v2, /device:TPU:0, one launch (start us, length us, event | category | flops | bytes accessed | tf_op | source)
XLA Modules:
  0.0 65.4 jit_solution(8525636464423238042)
XLA Ops:
  0.0 1.4 %copy.7.routes_ref = s32[128,8]{1,0:T(8,128)} copy(s32[128,8]{0,1:T(8,128)} %param.8) | data formatting | bytes 8192 | tf_op args[2]
  1.4 62.4 %project_and_sum.1 = f32[8,4096]{1,0:T(8,128)} custom-call(bf16[128,2048]{1,0:T(8,128)(2,1)} %tok_hbm.1, bf16[1024,1024]{1,0:T(8,128)(2,1)} %bitcast.4, s32[128,8]{1,0:T(8,128)} %copy.7.routes_ref, s32[1,128]{1,0:T(1,128)} %bitcast.7, bf16[256,2048]{1,0:T(8,128)(2,1)} %bitcast.5, bf16[256,1024]{1,0:T(8,128)(2,1)} %bitcast.6), custom_call_target="tpu_custom_call" | custom-call | flops 5368709120 | bytes 16777216 | tf_op jit(solution)/shard_map/project_and_sum/pallas_call | solution.py:346
  63.9 1.6 %copy.9 = f32[8,4096]{1,0:T(8,128)} copy(f32[8,4096]{1,0:T(8,128)} %project_and_sum.1) | data formatting | bytes 262144

commit v3 on v2

--- a/solution.py
+++ b/solution.py
@@ -11,10 +11,55 @@
 MESH = pl.DeviceIdType.MESH
 LO, HI, XP, CORE, YP = range(5)
 NT = (((1,), (1,)), ((), ()))
-FULL_IN = (1,)
-
-
-def kernel(zn, yn, tok_hbm, grad_hbm, routes_ref, doc_ref, win_hbm, wgr_hbm, out_ref,
+FULL_IN = (3,)
+FULL_GR = (1,)
+FULL_Y = (0, 1)
+FIRST_Z = ("in", "gr")
+FIRST_Y = ("gr", "tok")
+
+
+def order_of(zn, yn):
+    if (zn, yn) == (4, 2):
+        return ORDER
+    order = [("K", "gr", 0, 1, 0), ("T", 0, 1)]
+    if yn == 2:
+        order += [("Y", 0, 1), ("K", "gr", 0, 1, 1)]
+    for d in range(1, zn):
+        for s in (1, -1):
+            order += [("Z", "gr", d, s), ("Z", "in", d, s)]
+        for s in (1, -1):
+            order += [("X", "gr", d, s, 0), ("X", "in", d, s, 0)]
+            if yn == 2:
+                order += [("Y", d, s), ("X", "gr", d, s, 1)]
+        for s in (1, -1):
+            order += [("K", "gr", d, s, 0), ("K", "in", d, s, 0)]
+            if yn == 2:
+                order += [("K", "gr", d, s, 1)]
+    if yn == 2:
+        order += [("F", d, s) for d in range(zn) for s in ((1, -1) if d else (1,))]
+    return order
+
+
+ORDER = [
+    ("Y", 0, 1), ("X", "gr", 1, 1, 1), ("Z", "in", 1, 1), ("Z", "gr", 1, -1), ("Z", "in", 1, -1),
+    ("Z", "gr", 2, -1), ("K", "gr", 1, -1, 0), ("Z", "gr", 1, 1), ("X", "in", 3, -1, 0),
+    ("K", "gr", 0, 1, 1), ("X", "in", 1, 1, 0), ("X", "in", 3, 1, 0), ("Z", "in", 2, 1),
+    ("X", "gr", 2, -1, 0), ("Z", "gr", 2, 1), ("Z", "in", 2, -1), ("T", 0, 1), ("Y", 1, -1),
+    ("K", "in", 1, 1, 0), ("K", "gr", 1, -1, 1), ("X", "in", 2, 1, 0), ("X", "gr", 1, -1, 0),
+    ("K", "gr", 2, -1, 0), ("Y", 2, -1), ("X", "in", 2, -1, 0), ("Z", "gr", 3, -1),
+    ("X", "in", 1, -1, 0), ("K", "gr", 0, 1, 0), ("X", "gr", 2, -1, 1), ("K", "in", 2, -1, 0),
+    ("K", "gr", 1, 1, 0), ("Y", 2, 1), ("Z", "gr", 3, 1), ("Y", 3, -1), ("Y", 1, 1),
+    ("K", "in", 1, -1, 0), ("F", 0, 1), ("K", "in", 2, 1, 0), ("Z", "in", 3, -1), ("F", 2, -1),
+    ("X", "gr", 3, -1, 0), ("K", "gr", 2, -1, 1), ("X", "gr", 2, 1, 1), ("K", "gr", 1, 1, 1),
+    ("F", 1, -1), ("Y", 3, 1), ("K", "in", 3, -1, 0), ("K", "gr", 2, 1, 1), ("Z", "in", 3, 1),
+    ("F", 1, 1), ("X", "gr", 1, 1, 0), ("X", "gr", 3, -1, 1), ("X", "gr", 1, -1, 1),
+    ("K", "gr", 3, -1, 0), ("X", "gr", 2, 1, 0), ("K", "gr", 3, -1, 1), ("X", "gr", 3, 1, 0),
+    ("F", 2, 1), ("K", "in", 3, 1, 0), ("K", "gr", 2, 1, 0), ("X", "gr", 3, 1, 1),
+    ("K", "gr", 3, 1, 0), ("K", "gr", 3, 1, 1), ("F", 3, 1), ("F", 3, -1),
+]
+
+
+def kernel(zn, yn, order, tok_hbm, grad_hbm, routes_ref, doc_ref, win_hbm, wgr_hbm, out_ref,
            tok, grads, win, wgr, feat_send, feat_recv, acc_in, acc_gr, route_at,
            local_sem, in_recv, gr_recv, in_send, gr_send,
            tok_send_sem, tok_recv_sem, feat_send_sem, feat_recv_sem):
@@ -121,12 +166,14 @@
                 device_id=to[CORE], device_id_type=MESH).wait_recv()
         when([valid(d, sign)], wait)
 
+    full_z = {"in": FULL_IN, "gr": FULL_GR}
+
     def z_event(kind, d, sign):
         link = LO if sign > 0 else HI
+        full = d in full_z[kind]
         arrive(kind, d, sign, 0, 0)
         if d < last:
             send_piece(kind, d, sign, 0, 0, link)
-        full = kind == "in" and d in FULL_IN
         if kind == "gr" and yn == 2:
             send_piece(kind, d, sign, 0, 0, YP)
         if not full:
@@ -134,26 +181,32 @@
         send_piece(kind, d, sign, 0, 0, CORE)
         if full:
             arrive(kind, d, sign, 0, 1)
-            if d < last and d + 1 in FULL_IN:
-                send_piece(kind, d, sign, 0, 1, link)
-            send_piece(kind, d, sign, 0, 1, CORE)
+            other_half(kind, d, sign)
+
+    def other_half(kind, d, sign):
+        if d < last and d + 1 in full_z[kind]:
+            send_piece(kind, d, sign, 0, 1, LO if sign > 0 else HI)
+        if kind == "gr" and yn == 2 and d in FULL_Y:
+            send_piece(kind, d, sign, 0, 1, YP)
+        send_piece(kind, d, sign, 0, 1, CORE)
 
     def y_event(d, sign):
         arrive("gr", d, sign, 1, 0)
-        if d > 0:
+        if d not in FULL_Y:
             send_piece("gr", d, sign, 1, 0, XP)
         send_piece("gr", d, sign, 1, 0, CORE)
-        if d == 0:
+        if d in FULL_Y:
             arrive("gr", d, sign, 1, 1)
             send_piece("gr", d, sign, 1, 1, CORE)
 
     def x_event(kind, d, sign, yr):
-        if kind == "in" and d in FULL_IN:
+        if d in (full_z[kind] if yr == 0 else FULL_Y):
             return
         arrive(kind, d, sign, yr, 1)
-        if kind == "in" and d < last and d + 1 in FULL_IN:
-            send_piece(kind, d, sign, yr, 1, LO if sign > 0 else HI)
-        send_piece(kind, d, sign, yr, 1, CORE)
+        if yr == 0:
+            other_half(kind, d, sign)
+        else:
+            send_piece(kind, d, sign, yr, 1, CORE)
 
     def core_event(kind, d, sign, yr):
         arrive(kind, d, sign, yr, 0, 1)
@@ -219,20 +272,25 @@
             select_inputs(slot * yn + 1 - y, feat_recv.at[slot])
         when([valid(d, sign)], run)
 
-    for link in (LO, HI):
-        send_piece("gr", 0, 1, 0, 0, link)
-        send_piece("in", 0, 1, 0, 0, link)
-        if 1 in FULL_IN:
-            send_piece("in", 0, 1, 0, 1, link)
+    def make_tok():
+        return pltpu.make_async_remote_copy(
+            src_ref=tok_hbm, dst_ref=tok.at[pl.ds(tokens, tokens)],
+            send_sem=tok_send_sem, recv_sem=tok_recv_sem,
+            device_id=to[YP], device_id_type=MESH)
+
+    for kind in FIRST_Z:
+        for link in (LO, HI):
+            send_piece(kind, 0, 1, 0, 0, link)
+            if 1 in full_z[kind]:
+                send_piece(kind, 0, 1, 0, 1, link)
     if yn == 2:
-        def make_tok():
-            return pltpu.make_async_remote_copy(
-                src_ref=tok_hbm, dst_ref=tok.at[pl.ds(tokens, tokens)],
-                send_sem=tok_send_sem, recv_sem=tok_recv_sem,
-                device_id=to[YP], device_id_type=MESH)
-        send(make_tok, [])
-        send_piece("gr", 0, 1, 0, 0, YP)
-        send_piece("gr", 0, 1, 0, 1, YP)
+        for what in FIRST_Y:
+            if what == "tok":
+                send(make_tok, [])
+                continue
+            send_piece("gr", 0, 1, 0, 0, YP)
+            if 0 in FULL_Y:
+                send_piece("gr", 0, 1, 0, 1, YP)
 
     pair = lax.broadcasted_iota(jnp.int32, (pairs, tokens), 0) // fan
     spread = (pair == lax.broadcasted_iota(jnp.int32, (pairs, tokens), 1)).astype(jnp.bfloat16)
@@ -247,64 +305,31 @@
     for c in local:
         c.wait()
 
-    signs = (1, -1)
-    other = tuple(range(1, yn))
-    project_grads(0, 1, 0)
-    for d in range(1, zn):
-        for s in signs:
-            z_event("gr", d, s)
-        if d > 1:
-            for s in signs:
-                x_event("in", d - 1, s, 0)
-        for s in signs:
-            z_event("in", d, s)
-        if d == 1:
+    def run_event(event):
+        what = event[0]
+        if what == "Z":
+            z_event(*event[1:])
+        elif what == "X":
+            x_event(*event[1:])
+        elif what == "Y":
+            y_event(*event[1:])
+        elif what == "F":
+            features_back(*event[1:])
+        elif what == "T":
             if yn == 2:
                 make_tok().wait_recv()
             project_inputs(0, 1)
-            if yn == 2:
-                y_event(0, 1)
-                core_event("gr", 0, 1, 1)
-                project_grads(0, 1, 1)
-            features_back(0, 1)
-        for s in signs:
-            x_event("gr", d, s, 0)
-        for e in other:
-            for s in signs:
-                y_event(d, s)
-        if d > 1:
-            for s in signs:
-                core_event("in", d - 1, s, 0)
-                project_inputs(d - 1, s)
-            for s in signs:
-                core_event("gr", d - 1, s, 0)
-                project_grads(d - 1, s, 0)
-            for e in other:
-                for s in signs:
-                    x_event("gr", d - 1, s, e)
-            for e in other:
-                for s in signs:
-                    core_event("gr", d - 1, s, e)
-                    project_grads(d - 1, s, e)
-            for s in signs:
-                features_back(d - 1, s)
-    for s in signs:
-        x_event("in", last, s, 0)
-    for e in other:
-        for s in signs:
-            x_event("gr", last, s, e)
-    for s in signs:
-        core_event("gr", last, s, 0)
-        project_grads(last, s, 0)
-    for s in signs:
-        core_event("in", last, s, 0)
-        project_inputs(last, s)
-    for e in other:
-        for s in signs:
-            core_event("gr", last, s, e)
-            project_grads(last, s, e)
-    for s in signs:
-        features_back(last, s)
+        else:
+            kind, d, sign, yr = event[1:]
+            if (d, yr) != (0, 0):
+                core_event(kind, d, sign, yr)
+            if kind == "in":
+                project_inputs(d, sign)
+            else:
+                project_grads(d, sign, yr)
+
+    for event in order:
+        run_event(event)
 
     right = acc_in[...]
     right = (right + pltpu.roll(right, 64, 1)).astype(jnp.bfloat16)
@@ -344,7 +369,7 @@
     hbm = pl.BlockSpec(memory_space=pl.ANY)
     dma = pltpu.SemaphoreType.DMA
     return pl.pallas_call(
-        functools.partial(kernel, zn, yn),
+        functools.partial(kernel, zn, yn, order_of(zn, yn)),
         out_shape=jax.ShapeDtypeStruct((DOC_DEV, rank * rank), jnp.float32),
         in_specs=[hbm, hbm, vmem, vmem, hbm, hbm],
         out_specs=vmem,

time: 65.6 us -> 53.7 us (0.82)
  Pallas kernels: 62.4 us -> 50.5 us
    pallas_call x1, Pallas kernels: 62.4 us -> 50.5 us  [shards(): pl.pallas_call(functools.partial(kernel, zn, yn, order_of(zn, yn)), out_s...]
where the time goes in v3:
time: 53.7 us; the launch traced here: 53.5 us
  Pallas kernels  50.5 us (94%)
  local copies, waits for them, and re-layouts  2.98 us (6%)
    pallas_call x1, Pallas kernels, shards(): pl.pallas_call(functools.partial(kernel, zn, yn, order_of(zn, yn)), out_s...  50.5 us
    unnamed x2, local copies, waits for them, and re-layouts  2.98 us

profile of v3, /device:TPU:0, one launch (start us, length us, event | category | flops | bytes accessed | tf_op | source)
XLA Modules:
  0.0 53.5 jit_solution(10689603429396375249)
XLA Ops:
  0.0 1.4 %copy.7.routes_ref = s32[128,8]{1,0:T(8,128)} copy(s32[128,8]{0,1:T(8,128)} %param.8) | data formatting | bytes 8192 | tf_op args[2]
  1.4 50.5 %project_and_sum.1 = f32[8,4096]{1,0:T(8,128)} custom-call(bf16[128,2048]{1,0:T(8,128)(2,1)} %tok_hbm.1, bf16[1024,1024]{1,0:T(8,128)(2,1)} %bitcast.4, s32[128,8]{1,0:T(8,128)} %copy.7.routes_ref, s32[1,128]{1,0:T(1,128)} %bitcast.7, bf16[256,2048]{1,0:T(8,128)(2,1)} %bitcast.5, bf16[256,1024]{1,0:T(8,128)(2,1)} %bitcast.6), custom_call_target="tpu_custom_call" | custom-call | flops 5368709120 | bytes 16777216 | tf_op jit(solution)/shard_map/project_and_sum/pallas_call | solution.py:371
  51.9 1.6 %copy.9 = f32[8,4096]{1,0:T(8,128)} copy(f32[8,4096]{1,0:T(8,128)} %project_and_sum.1) | data formatting | bytes 262144

commit v4 on v3

--- a/solution.py
+++ b/solution.py
@@ -11,11 +11,11 @@
 MESH = pl.DeviceIdType.MESH
 LO, HI, XP, CORE, YP = range(5)
 NT = (((1,), (1,)), ((), ()))
-FULL_IN = (3,)
-FULL_GR = (1,)
-FULL_Y = (0, 1)
-FIRST_Z = ("in", "gr")
-FIRST_Y = ("gr", "tok")
+FULL_IN = ((3,), (1, 3))
+FULL_GR = ()
+FULL_Y = (0, 2)
+FIRST_Z = ("gr", "ia", "ib")
+FIRST_Y = ("tok", "g0", "g1")
 
 
 def order_of(zn, yn):
@@ -26,9 +26,9 @@
         order += [("Y", 0, 1), ("K", "gr", 0, 1, 1)]
     for d in range(1, zn):
         for s in (1, -1):
-            order += [("Z", "gr", d, s), ("Z", "in", d, s)]
+            order += [("Z", "gr", d, s), ("Z", "ia", d, s), ("Z", "ib", d, s)]
         for s in (1, -1):
-            order += [("X", "gr", d, s, 0), ("X", "in", d, s, 0)]
+            order += [("X", "gr", d, s, 0), ("X", "ia", d, s, 0), ("X", "ib", d, s, 0)]
             if yn == 2:
                 order += [("Y", d, s), ("X", "gr", d, s, 1)]
         for s in (1, -1):
@@ -41,21 +41,24 @@
 
 
 ORDER = [
-    ("Y", 0, 1), ("X", "gr", 1, 1, 1), ("Z", "in", 1, 1), ("Z", "gr", 1, -1), ("Z", "in", 1, -1),
-    ("Z", "gr", 2, -1), ("K", "gr", 1, -1, 0), ("Z", "gr", 1, 1), ("X", "in", 3, -1, 0),
-    ("K", "gr", 0, 1, 1), ("X", "in", 1, 1, 0), ("X", "in", 3, 1, 0), ("Z", "in", 2, 1),
-    ("X", "gr", 2, -1, 0), ("Z", "gr", 2, 1), ("Z", "in", 2, -1), ("T", 0, 1), ("Y", 1, -1),
-    ("K", "in", 1, 1, 0), ("K", "gr", 1, -1, 1), ("X", "in", 2, 1, 0), ("X", "gr", 1, -1, 0),
-    ("K", "gr", 2, -1, 0), ("Y", 2, -1), ("X", "in", 2, -1, 0), ("Z", "gr", 3, -1),
-    ("X", "in", 1, -1, 0), ("K", "gr", 0, 1, 0), ("X", "gr", 2, -1, 1), ("K", "in", 2, -1, 0),
-    ("K", "gr", 1, 1, 0), ("Y", 2, 1), ("Z", "gr", 3, 1), ("Y", 3, -1), ("Y", 1, 1),
-    ("K", "in", 1, -1, 0), ("F", 0, 1), ("K", "in", 2, 1, 0), ("Z", "in", 3, -1), ("F", 2, -1),
-    ("X", "gr", 3, -1, 0), ("K", "gr", 2, -1, 1), ("X", "gr", 2, 1, 1), ("K", "gr", 1, 1, 1),
-    ("F", 1, -1), ("Y", 3, 1), ("K", "in", 3, -1, 0), ("K", "gr", 2, 1, 1), ("Z", "in", 3, 1),
-    ("F", 1, 1), ("X", "gr", 1, 1, 0), ("X", "gr", 3, -1, 1), ("X", "gr", 1, -1, 1),
-    ("K", "gr", 3, -1, 0), ("X", "gr", 2, 1, 0), ("K", "gr", 3, -1, 1), ("X", "gr", 3, 1, 0),
-    ("F", 2, 1), ("K", "in", 3, 1, 0), ("K", "gr", 2, 1, 0), ("X", "gr", 3, 1, 1),
-    ("K", "gr", 3, 1, 0), ("K", "gr", 3, 1, 1), ("F", 3, 1), ("F", 3, -1),
+    ("Z", "gr", 1, -1), ("Z", "gr", 1, 1), ("Z", "ia", 1, 1), ("Z", "ib", 1, 1), ("Z", "ia", 1, -1),
+    ("T", 0, 1), ("X", "gr", 1, -1, 0), ("Z", "ib", 1, -1), ("Z", "gr", 2, -1), ("Z", "ia", 2, -1),
+    ("X", "ia", 1, 1, 0), ("Z", "gr", 2, 1), ("X", "gr", 2, -1, 0), ("Z", "ib", 2, -1),
+    ("X", "ib", 3, -1, 0), ("Y", 0, 1), ("X", "gr", 2, 1, 1), ("Z", "ia", 2, 1),
+    ("K", "gr", 1, -1, 0), ("K", "gr", 0, 1, 0), ("X", "ia", 3, 1, 0), ("Z", "gr", 3, -1),
+    ("K", "gr", 0, 1, 1), ("Y", 1, -1), ("Z", "ib", 2, 1), ("X", "ib", 2, -1, 0),
+    ("X", "gr", 2, -1, 1), ("Z", "gr", 3, 1), ("X", "ia", 2, -1, 0), ("X", "gr", 1, 1, 0),
+    ("X", "ia", 1, -1, 0), ("Y", 1, 1), ("X", "gr", 2, 1, 0), ("K", "in", 1, -1, 0),
+    ("X", "gr", 3, -1, 0), ("K", "in", 1, 1, 0), ("F", 0, 1), ("X", "gr", 3, 1, 0),
+    ("K", "gr", 2, -1, 0), ("K", "gr", 2, 1, 0), ("Y", 3, 1), ("X", "ia", 2, 1, 0),
+    ("X", "ib", 2, 1, 0), ("Y", 3, -1), ("K", "gr", 1, 1, 0), ("K", "in", 2, 1, 0),
+    ("X", "gr", 1, 1, 1), ("Z", "ia", 3, 1), ("Y", 2, 1), ("X", "gr", 1, -1, 1),
+    ("K", "gr", 2, 1, 1), ("Z", "ib", 3, 1), ("X", "ib", 1, 1, 0), ("K", "in", 2, -1, 0),
+    ("Y", 2, -1), ("Z", "ib", 3, -1), ("K", "gr", 1, -1, 1), ("X", "ia", 3, -1, 0), ("F", 1, 1),
+    ("F", 1, -1), ("K", "in", 3, 1, 0), ("K", "gr", 3, -1, 0), ("K", "gr", 3, 1, 0),
+    ("X", "ib", 1, -1, 0), ("Z", "ia", 3, -1), ("K", "gr", 2, -1, 1), ("X", "gr", 3, 1, 1),
+    ("K", "in", 3, -1, 0), ("F", 2, 1), ("K", "gr", 1, 1, 1), ("F", 2, -1), ("X", "gr", 3, -1, 1),
+    ("K", "gr", 3, -1, 1), ("K", "gr", 3, 1, 1), ("F", 3, 1), ("F", 3, -1), ("X", "ib", 3, 1, 0),
 ]
 
 
@@ -72,6 +75,8 @@
     pairs = grad_hbm.shape[0]
     cols = win.shape[1]
     part = cols // 4
+    size = {"gr": part, "ia": part // 2, "ib": part // 2}
+    skip = {"gr": 0, "ia": 0, "ib": part // 2}
     last = zn - 1
     to = {
         LO: {"expert": place - yn},
@@ -128,36 +133,40 @@
         when(conds, lambda: make().start())
         sent.append((make, conds))
 
-    def rows_of(dh, dc=0):
+    def rows_of(kind, dh, dc=0):
         half = hx if dh == 0 else 1 - hx
         which = core if dc == 0 else 1 - core
-        return pl.ds(pl.multiple_of((half * 2 + which) * part, part), part), half * 2 + which
+        number = half * 2 + which
+        start = pl.multiple_of(number * part + skip[kind], part // 2)
+        if kind == "ib":
+            number += 4
+        return pl.ds(start, size[kind]), number
 
     def pack(kind, d, sign, yr):
         zz = z + sign * d
-        if kind == "in":
+        if kind != "gr":
             return win, zz, in_send, in_recv
         yy = y if yr == 0 else 1 - y
         return wgr, zz * yn + yy, gr_send, gr_recv
 
     def send_piece(kind, d, sign, yr, dh, link):
         buf, slot, ssem, rsem = pack(kind, d, sign, yr)
-        rows, number = rows_of(dh)
+        rows, number = rows_of(kind, dh)
         if d == 0 and yr == 0:
-            src = (win_hbm if kind == "in" else wgr_hbm).at[rows]
+            src = (wgr_hbm if kind == "gr" else win_hbm).at[rows]
         else:
             src = buf.at[slot, rows]
 
         def make():
             return pltpu.make_async_remote_copy(
                 src_ref=src, dst_ref=buf.at[slot, rows],
-                send_sem=ssem.at[link, slot, dh], recv_sem=rsem.at[slot, number],
+                send_sem=ssem.at[link, slot, dh + 2 * (kind == "ib")], recv_sem=rsem.at[slot, number],
                 device_id=to[link], device_id_type=MESH)
         send(make, [valid(d, sign), have(link)])
 
     def arrive(kind, d, sign, yr, dh, dc=0):
         buf, slot, ssem, rsem = pack(kind, d, sign, yr)
-        rows, number = rows_of(dh, dc)
+        rows, number = rows_of(kind, dh, dc)
 
         def wait():
             pltpu.make_async_remote_copy(
@@ -166,7 +175,7 @@
                 device_id=to[CORE], device_id_type=MESH).wait_recv()
         when([valid(d, sign)], wait)
 
-    full_z = {"in": FULL_IN, "gr": FULL_GR}
+    full_z = {"ia": FULL_IN[0], "ib": FULL_IN[1], "gr": FULL_GR}
 
     def z_event(kind, d, sign):
         link = LO if sign > 0 else HI
@@ -209,8 +218,9 @@
             send_piece(kind, d, sign, yr, 1, CORE)
 
     def core_event(kind, d, sign, yr):
-        arrive(kind, d, sign, yr, 0, 1)
-        arrive(kind, d, sign, yr, 1, 1)
+        for piece in ("gr",) if kind == "gr" else ("ia", "ib"):
+            arrive(piece, d, sign, yr, 0, 1)
+            arrive(piece, d, sign, yr, 1, 1)
 
     tile = 256
 
@@ -244,7 +254,7 @@
             select(acc_in, at, slot, value)
 
     def project_inputs(d, sign):
-        _, slot, _, _ = pack("in", d, sign, 0)
+        _, slot, _, _ = pack("ia", d, sign, 0)
 
         def run():
             value = lax.dot_general(tok[...], win[slot], NT, preferred_element_type=jnp.float32)
@@ -262,7 +272,7 @@
     def features_back(d, sign):
         if yn == 1:
             return
-        _, slot, _, _ = pack("in", d, sign, 0)
+        _, slot, _, _ = pack("ia", d, sign, 0)
 
         def run():
             pltpu.make_async_remote_copy(
@@ -288,13 +298,15 @@
             if what == "tok":
                 send(make_tok, [])
                 continue
-            send_piece("gr", 0, 1, 0, 0, YP)
-            if 0 in FULL_Y:
+            if what == "g0":
+                send_piece("gr", 0, 1, 0, 0, YP)
+            elif 0 in FULL_Y:
                 send_piece("gr", 0, 1, 0, 1, YP)
 
     pair = lax.broadcasted_iota(jnp.int32, (pairs, tokens), 0) // fan
     spread = (pair == lax.broadcasted_iota(jnp.int32, (pairs, tokens), 1)).astype(jnp.bfloat16)
-    named = jnp.dot(spread, routes_ref[...].astype(jnp.bfloat16), preferred_element_type=jnp.float32)
+    named = lax.dot_general(spread, routes_ref[...].astype(jnp.bfloat16), NT,
+                            preferred_element_type=jnp.float32)
     choice = lax.broadcasted_iota(jnp.int32, (pairs, fan), 0) % fan
     mine = choice == lax.broadcasted_iota(jnp.int32, (pairs, fan), 1)
     named = jnp.sum(jnp.where(mine, named, 0.0), axis=1, keepdims=True).astype(jnp.int32)
@@ -384,9 +396,9 @@
             pltpu.VMEM((pairs, 128), jnp.float32),
             pltpu.VMEM((pairs, 128), jnp.int32),
             dma((4,)),
-            dma((zn, 4)),
+            dma((zn, 8)),
             dma((zn * yn, 4)),
-            dma((4, zn, 2)),
+            dma((4, zn, 4)),
             dma((5, zn * yn, 2)),
             dma,
             dma,
@@ -399,7 +411,7 @@
             flops=2 * pairs * hidden * cols * zn * yn + 2 * tok * yn * width * cols * zn,
             bytes_accessed=16 * 2**20, transcendentals=0),
         name="project_and_sum",
-    )(tokens, grad_rows.reshape(pairs, hidden), routes, doc_ids.reshape(1, tok),
+    )(tokens, grad_rows.reshape(pairs, hidden), routes.T, doc_ids.reshape(1, tok),
       input_proj.reshape(cols, width), grad_proj.reshape(cols, hidden))
 
 

time: 53.7 us -> 54 us (level)
  Pallas kernels: 50.5 us -> 52.2 us
  local copies, waits for them, and re-layouts: 2.98 us -> 1.57 us
    pallas_call x1, Pallas kernels: 50.5 us -> 52.2 us  [shards(): pl.pallas_call(functools.partial(kernel, zn, yn, order_of(zn, yn)), out_s...]
    unnamed x2 -> x1, local copies, waits for them, and re-layouts: 2.98 us -> 1.57 us
where the time goes in v4:
time: 54 us; the launch traced here: 53.8 us
  Pallas kernels  52.2 us (97%)
  local copies, waits for them, and re-layouts  1.57 us (3%)
    pallas_call x1, Pallas kernels, shards(): pl.pallas_call(functools.partial(kernel, zn, yn, order_of(zn, yn)), out_s...  52.2 us
    unnamed x1, local copies, waits for them, and re-layouts  1.57 us

profile of v4, /device:TPU:0, one launch (start us, length us, event | category | flops | bytes accessed | tf_op | source)
XLA Modules:
  0.0 53.8 jit_solution(3874670012630817506)
XLA Ops:
  0.0 52.2 %project_and_sum.1 = f32[8,4096]{1,0:T(8,128)} custom-call(bf16[128,2048]{1,0:T(8,128)(2,1)} %tok_hbm.1, bf16[1024,1024]{1,0:T(8,128)(2,1)} %bitcast.5, s32[8,128]{1,0:T(8,128)} %bitcast.8, s32[1,128]{1,0:T(1,128)} %bitcast.9, bf16[256,2048]{1,0:T(8,128)(2,1)} %bitcast.6, bf16[256,1024]{1,0:T(8,128)(2,1)} %bitcast.7), custom_call_target="tpu_custom_call" | custom-call | flops 5368709120 | bytes 16777216 | tf_op jit(solution)/shard_map/project_and_sum/pallas_call | solution.py:383
  52.2 1.6 %copy.8 = f32[8,4096]{1,0:T(8,128)} copy(f32[8,4096]{1,0:T(8,128)} %project_and_sum.1) | data formatting | bytes 262144

commit v5 on v3

--- a/solution.py
+++ b/solution.py
@@ -294,7 +294,8 @@
 
     pair = lax.broadcasted_iota(jnp.int32, (pairs, tokens), 0) // fan
     spread = (pair == lax.broadcasted_iota(jnp.int32, (pairs, tokens), 1)).astype(jnp.bfloat16)
-    named = jnp.dot(spread, routes_ref[...].astype(jnp.bfloat16), preferred_element_type=jnp.float32)
+    named = lax.dot_general(spread, routes_ref[...].astype(jnp.bfloat16), NT,
+                            preferred_element_type=jnp.float32)
     choice = lax.broadcasted_iota(jnp.int32, (pairs, fan), 0) % fan
     mine = choice == lax.broadcasted_iota(jnp.int32, (pairs, fan), 1)
     named = jnp.sum(jnp.where(mine, named, 0.0), axis=1, keepdims=True).astype(jnp.int32)
@@ -399,7 +400,7 @@
             flops=2 * pairs * hidden * cols * zn * yn + 2 * tok * yn * width * cols * zn,
             bytes_accessed=16 * 2**20, transcendentals=0),
         name="project_and_sum",
-    )(tokens, grad_rows.reshape(pairs, hidden), routes, doc_ids.reshape(1, tok),
+    )(tokens, grad_rows.reshape(pairs, hidden), routes.T, doc_ids.reshape(1, tok),
       input_proj.reshape(cols, width), grad_proj.reshape(cols, hidden))
 
 

time: 53.7 us -> 52.1 us (0.970)
  local copies, waits for them, and re-layouts: 2.98 us -> 1.57 us
    unnamed x2 -> x1, local copies, waits for them, and re-layouts: 2.98 us -> 1.57 us
where the time goes in v5:
time: 52.1 us; the launch traced here: 51.9 us
  Pallas kernels  50.4 us (97%)
  local copies, waits for them, and re-layouts  1.57 us (3%)
    pallas_call x1, Pallas kernels, shards(): pl.pallas_call(functools.partial(kernel, zn, yn, order_of(zn, yn)), out_s...  50.4 us
    unnamed x1, local copies, waits for them, and re-layouts  1.57 us

profile of v5, /device:TPU:0, one launch (start us, length us, event | category | flops | bytes accessed | tf_op | source)
XLA Modules:
  0.0 51.9 jit_solution(5972270755338235768)
XLA Ops:
  0.0 50.4 %project_and_sum.1 = f32[8,4096]{1,0:T(8,128)} custom-call(bf16[128,2048]{1,0:T(8,128)(2,1)} %tok_hbm.1, bf16[1024,1024]{1,0:T(8,128)(2,1)} %bitcast.5, s32[8,128]{1,0:T(8,128)} %bitcast.8, s32[1,128]{1,0:T(1,128)} %bitcast.9, bf16[256,2048]{1,0:T(8,128)(2,1)} %bitcast.6, bf16[256,1024]{1,0:T(8,128)(2,1)} %bitcast.7), custom_call_target="tpu_custom_call" | custom-call | flops 5368709120 | bytes 16777216 | tf_op jit(solution)/shard_map/project_and_sum/pallas_call | solution.py:372
  50.4 1.6 %copy.8 = f32[8,4096]{1,0:T(8,128)} copy(f32[8,4096]{1,0:T(8,128)} %project_and_sum.1) | data formatting | bytes 262144
